TPU v7x, 256 devices: a whole 4x4x8 slice. The times are simulated.
256 devices in a mesh: pair: 32 (over y, z), virt: 8 (over x, core).
Axes of the slice: x: 4, y: 4, z: 8, core: 2. Of those that a mesh axis runs over, the one named last changes fastest.
Arguments:
- amplitudes: bfloat16 [16384, 16, 2048], P('pair', None, 'virt'), may hold values from -6 to 6
- integrals: bfloat16 [1024, 16, 2048], P(None, None, 'virt'), may hold values from -0.09375 to 0.09375
- mask: int32 [16384, 16, 16], P('pair', None, 'virt'), may hold values from 0 to 1
- slab: int32 [1], replicated, may hold values from 0 to 127
- owner: int32 [16384], replicated, may hold values from 0 to 16383, as said below
Outputs:
- symmetric: float32 [16384, 1024], P('pair', 'virt')
Inputs may be any that keep to these rules, and one draw needn't show every extreme that they name: owner is a permutation; ids 2 q and 2 q + 1 are a pair ij and its mirror ji, never on the same index of pair; for any two indices of pair, at most 17 slots of one hold pairs whose mirror sits on the other, and this is reached.
All inputs are finite; a program needn't handle non-finite values.
Results may differ from a plain program's by a relative error of at most 0.0003.
Values sent between devices are 32-bit elements; how exact they have to be, the bound alone decides.
A program may use at most 64 MiB of HBM per device.

v0:
```python
import jax
import jax.numpy as jnp
from jax import lax
from jax.sharding import PartitionSpec as P

TILE = 128
CSLAB = 16
WA = 32


def per_device(amplitudes, integrals, mask, slab, owner):
    rows_here = amplitudes.shape[0]
    local_tiles = mask.shape[2]
    slab_tile = slab[0] * CSLAB // TILE
    tile_iota = jnp.arange(mask.shape[1], dtype=jnp.int32)
    tile_hit = (tile_iota == slab_tile).astype(jnp.int32)
    picked = jnp.sum(mask * tile_hit[None, :, None], axis=1)
    picked_soft = picked.astype(amplitudes.dtype)
    width_here = amplitudes.shape[2]
    tiled = amplitudes.reshape(rows_here, CSLAB, local_tiles, width_here // local_tiles)
    masked = (tiled * picked_soft[:, None, :, None]).reshape(rows_here, CSLAB, width_here)
    partial_value = jnp.einsum("pcd,rcd->pr", masked, integrals, preferred_element_type=jnp.float32)
    block_width = WA
    count_virt = lax.axis_size("virt")
    share_size = block_width // count_virt
    own_rows = lax.psum_scatter(partial_value, "virt", scatter_dimension=1, tiled=True)
    blocks = own_rows.reshape(rows_here, share_size, count_virt, share_size)
    turned = lax.all_to_all(blocks, "virt", split_axis=2, concat_axis=1, tiled=True)
    swapped = (
        turned.reshape(rows_here, block_width, share_size)
        .transpose(0, 2, 1)
        .reshape(rows_here, share_size * block_width)
    )
    everything = owner.shape[0]
    slot_ids = jnp.arange(everything, dtype=jnp.int32)
    self_index = lax.axis_index("pair")
    first_slot = self_index * rows_here
    my_owner = lax.dynamic_slice_in_dim(owner, first_slot, rows_here)
    wanted = jnp.bitwise_xor(my_owner, 1)
    matches = owner[None, :] == wanted[:, None]
    mirror_slots = jnp.sum(jnp.where(matches, slot_ids[None, :], 0), axis=1)
    gathered = lax.all_gather(swapped, "pair", axis=0, tiled=True)
    fetched = jnp.take(gathered, mirror_slots, axis=0)
    return own_rows + fetched


def solution(mesh):
    return jax.shard_map(
        per_device,
        mesh=mesh,
        in_specs=(
            P("pair", None, "virt"),
            P(None, None, "virt"),
            P("pair", None, "virt"),
            P(),
            P(),
        ),
        out_specs=P("pair", "virt"),
        check_vma=False,
    )
```

profile of v0, /device:TPU:1, one launch (start us, length us, event | category | flops | bytes accessed | tf_op | source)
XLA Modules:
  0.0 185.3 jit_solution(12174444571198599233)
XLA Ops:
  6.5 0.0 reduce-scatter.2.cloned.1.call-start
  7.2 0.9 multiply_reduce_fusion
  8.2 0.2 copy.21
  8.4 0.0 copy-start.1
  8.4 0.6 mul.34
  9.0 2.8 %broadcast_multiply_fusion = bf16[512,16,256]{2,1,0:T(8,128)(2,1)S(1)} fusion(bf16[512,16,256]{2,1,0:T(8,128)(2,1)} %param.5, bf16[512,256]{1,0:T(8,128)(2,1)S(1)} %bitcast.19), kind=kLoop, calls=%fused_computation.5 | loop fusion | flops 2097152 | bytes 8650752 | tf_op jit(solution)/shard_map/mul | solution.py:21
  11.9 1.2 copy-done.1
  13.0 0.0 copy-start
  13.0 9.2 %fusion.3 = f32[512,1024]{1,0:T(8,128)} fusion(bf16[1024,16,256]{2,1,0:T(8,128)(2,1)S(1)} %copy-done.1, bf16[512,16,256]{2,1,0:T(8,128)(2,1)S(1)} %broadcast_multiply_fusion), kind=kOutput, calls=%fused_computation.6 | convolution fusion | flops 4294967296 | bytes 14680064 | tf_op jit(solution)/shard_map/pcd,rcd->pr/dot_general | solution.py:22
  22.2 0.0 reduce-scatter.2.cloned.1.call-update
  22.3 0.0 all-gather.2.cloned.1.call-start
  22.3 37.4 %reduce-scatter.2.cloned.1.call-done = f32[512,128]{1,0:T(8,128)} async-done(((f32[512,1024]{1,0:T(8,128)}), f32[512,128]{1,0:T(8,128)}) %reduce-scatter.2.cloned.1.call-update) | async-done | bytes 262160 | tf_op jit(solution)/shard_map/reduce_scatter | solution.py:26
  59.8 1.1 copy.24
  60.8 0.1 reshape.43
  60.9 12.2 %all_to_all.15 = f32[512,4,8,4]{0,3,1,2:T(4,128)S(1)} all-to-all(f32[512,4,8,4]{0,3,1,2:T(4,128)S(1)} %copy.25), channel_id=1, replica_groups=mesh['pair'=32,'virt'=8] {'virt'}, dimensions={2} | all-to-all | bytes 524288 | tf_op jit(solution)/shard_map/all_to_all | solution.py:28
  73.1 0.1 copy.26
  73.2 0.8 copy.27
  74.1 0.0 all-gather.2.cloned.1.call-update
  74.1 0.0 copy-done
  74.1 0.1 dynamic-slice_xor_fusion
  74.2 4.6 %select_reduce_fusion = s32[512]{0:T(512)S(1)} fusion(s32[16384]{0:T(1024)S(1)} %copy-done, s32[512]{0:T(512)S(1)} %dynamic-slice_xor_fusion), kind=kLoop, calls=%fused_computation.1 | loop fusion | flops 25165312 | bytes 69632 | tf_op jit(solution)/shard_map/reduce_sum | solution.py:41
  78.9 93.3 %all-gather.2.cloned.1.call-done = f32[16384,128]{1,0:T(8,128)} async-done(((f32[512,128]{1,0:T(8,128)}), f32[16384,128]{1,0:T(8,128)}) %all-gather.2.cloned.1.call-update) | async-done | bytes 8388624 | tf_op jit(solution)/shard_map/all_gather | solution.py:42
  172.2 4.4 %gather_fusion = f32[512,128]{1,0:T(8,128)S(1)} fusion(f32[16384,128]{1,0:T(8,128)} %all-gather.2.cloned.1.call-done, s32[1024]{0:T(1024)S(1)} %pad_clamp_fusion), kind=kCustom, calls=%fused_computation | custom fusion | bytes 526336 | tf_op jit(solution)/shard_map/jit(_take)/gather | solution.py:43
  176.6 1.8 select_add_fusion
  (7 shorter events, 0.1 us)
Async XLA Ops:
  6.5 53.2 %reduce-scatter.2.cloned.1.call-start = ((), (), s32[]{:S(2)}) async-start(), calls=%async_computation.2 | async-start | bytes 2359296 | tf_op jit(solution)/shard_map/reduce_scatter | solution.py:26
  8.4 4.6 %copy-start.1 = (bf16[1024,16,256]{2,1,0:T(8,128)(2,1)S(1)}, bf16[1024,16,256]{2,1,0:T(8,128)(2,1)}, u32[]{:S(2)}) copy-start(bf16[1024,16,256]{2,1,0:T(8,128)(2,1)} %param.6) | copy-start | bytes 25165828
  13.0 61.1 %copy-start = (s32[16384]{0:T(1024)S(1)}, s32[16384]{0:T(1024)}, u32[]{:S(2)}) copy-start(s32[16384]{0:T(1024)} %param.9) | copy-start | bytes 196612
  22.3 150.0 %all-gather.2.cloned.1.call-start = ((), (), s32[]{:S(2)}) async-start(), calls=%async_computation.3 | async-start | bytes 8650752 | tf_op jit(solution)/shard_map/all_gather | solution.py:42
Sparse Core Ops, SparseCore 0:
  22.4 37.3 reduce-scatter.1
  74.2 97.9 all-gather.1
where the time goes:
time: 186 us; the launch traced here: 185 us
  waiting for transfers between devices  131 us (70%)
  between operations  14.2 us (8%)
  blocking collectives  12.2 us (7%)
  other arithmetic  10.3 us (6%)
  matrix products  9.21 us (5%)
  local copies, waits for them, and re-layouts  8.48 us (5%)
    all_gather x1, waiting for transfers between devices, per_device(): gathered = lax.all_gather(swapped, 'pair', axis=0, tiled=True)  93.3 us
    reduce_scatter x1, waiting for transfers between devices, per_device(): lax.psum_scatter(partial_value, 'virt', scatter_dimension=1, tiled=True)  37.4 us
    all_to_all x1, blocking collectives, per_device(): lax.all_to_all(blocks, 'virt', split_axis=2, concat_axis=1, tiled=True)  12.2 us
    dot_general x1, matrix products, per_device(): jnp.einsum('pcd,rcd->pr', masked, integrals, preferred_element_type=jnp.f...  9.21 us
    reduce_sum x1, other arithmetic, per_device(): mirror_slots = jnp.sum(jnp.where(matches, slot_ids[None, :], 0), axis=1)  4.65 us
    gather x1, local copies, waits for them, and re-layouts, per_device(): fetched = jnp.take(gathered, mirror_slots, axis=0)  4.41 us
  transfers between devices with their start and end apart: 2, of which 2 were waited for; matrix products, arithmetic and copies ran while one was open for 3% of the time, Pallas kernels for 0%

commit v1 on v0

v1 whole, which is shorter than its diff:
```python
import jax
import jax.numpy as jnp
from jax import lax
from jax.sharding import PartitionSpec as P

TILE = 128
CSLAB = 16
WA = 32
MOST = 17


def per_device(amplitudes, integrals, mask, slab, owner):
    rows_here = amplitudes.shape[0]
    local_tiles = mask.shape[2]
    slab_tile = slab[0] * CSLAB // TILE
    picked = lax.dynamic_index_in_dim(mask, slab_tile, axis=1, keepdims=False)
    picked_soft = picked.astype(amplitudes.dtype)
    width_here = amplitudes.shape[2]
    tiled = amplitudes.reshape(rows_here, CSLAB, local_tiles, width_here // local_tiles)
    masked = (tiled * picked_soft[:, None, :, None]).reshape(rows_here, CSLAB, width_here)
    partial_value = jnp.einsum("pcd,rcd->pr", masked, integrals, preferred_element_type=jnp.float32)
    count_virt = lax.axis_size("virt")
    count_pair = lax.axis_size("pair")
    share_size = WA // count_virt
    own_rows = lax.psum_scatter(partial_value, "virt", scatter_dimension=1, tiled=True)

    slot_ids = jnp.arange(owner.shape[0], dtype=jnp.int32)
    my_owner = lax.dynamic_slice_in_dim(owner, lax.axis_index("pair") * rows_here, rows_here)
    matches = owner[None, :] == jnp.bitwise_xor(my_owner, 1)[:, None]
    there = jnp.sum(jnp.where(matches, slot_ids[None, :] // rows_here, 0), axis=1)
    order = my_owner // 2
    before = (there[None, :] == there[:, None]) & (order[None, :] < order[:, None])
    place = there * MOST + jnp.sum(before.astype(jnp.int32), axis=1)
    places = jnp.arange(count_pair * MOST, dtype=jnp.int32)
    row_of = jnp.sum(jnp.where(place[:, None] == places[None, :], jnp.arange(rows_here, dtype=jnp.int32)[:, None], 0), axis=0)

    blocks = own_rows.reshape(rows_here, share_size, count_virt, share_size)
    turned = lax.all_to_all(blocks, "virt", split_axis=2, concat_axis=1, tiled=True)
    swapped = (
        turned.reshape(rows_here, WA, share_size)
        .transpose(0, 2, 1)
        .reshape(rows_here, share_size * WA)
    )
    sent = jnp.take(swapped, row_of, axis=0).reshape(count_pair, MOST, -1)
    came = lax.all_to_all(sent, "pair", split_axis=0, concat_axis=0, tiled=True)
    fetched = jnp.take(came.reshape(count_pair * MOST, -1), place, axis=0)
    return own_rows + fetched


def solution(mesh):
    return jax.shard_map(
        per_device,
        mesh=mesh,
        in_specs=(
            P("pair", None, "virt"),
            P(None, None, "virt"),
            P("pair", None, "virt"),
            P(),
            P(),
        ),
        out_specs=P("pair", "virt"),
        check_vma=False,
    )
```

time: 186 us -> 111 us (0.60)
  the two profiles are of different devices: /device:TPU:1 before, /device:TPU:32 now
where the time goes in v1:
time: 111 us
  waiting for transfers between devices  55.7 us (50%)
  between operations  14.2 us (13%)
  starting transfers between devices  13.5 us (12%)
  other arithmetic  10.3 us (9%)
  matrix products  9.21 us (8%)
  local copies, waits for them, and re-layouts  7.63 us (7%)
    reduce_scatter x1, waiting for transfers between devices, per_device(): lax.psum_scatter(partial_value, 'virt', scatter_dimension=1, tiled=True)  33.8 us
    all_to_all x1, waiting for transfers between devices, per_device(): came = lax.all_to_all(sent, 'pair', split_axis=0, concat_axis=0, tiled=True)  14.6 us
    all_to_all x1, starting transfers between devices, per_device(): came = lax.all_to_all(sent, 'pair', split_axis=0, concat_axis=0, tiled=True)  10.1 us
    dot_general x1, matrix products, per_device(): jnp.einsum('pcd,rcd->pr', masked, integrals, preferred_element_type=jnp.f...  9.21 us
    all_to_all x1, waiting for transfers between devices, per_device(): lax.all_to_all(blocks, 'virt', split_axis=2, concat_axis=1, tiled=True)  7.33 us
    reduce_sum x1, other arithmetic, per_device(): jnp.sum(jnp.where(matches, slot_ids[None, :] // rows_here, 0), axis=1)  4.43 us
    all_to_all x1, starting transfers between devices, per_device(): lax.all_to_all(blocks, 'virt', split_axis=2, concat_axis=1, tiled=True)  3.41 us
    mul x1, other arithmetic, per_device(): tiled * picked_soft[:, None, :, None]  2.7 us
  transfers between devices with their start and end apart: 3, of which 3 were waited for; matrix products, arithmetic and copies ran while one was open for 5% of the time, Pallas kernels for 0%

profile of v1, /device:TPU:32, one launch (start us, length us, event | category | flops | bytes accessed | tf_op | source)
XLA Modules:
  0.0 110.6 jit_solution(13117335480748077143)
XLA Ops:
  7.2 0.7 fusion.13
  7.9 0.2 copy.23
  8.1 0.6 mul.43
  8.8 2.7 %broadcast_multiply_fusion = bf16[512,16,256]{2,1,0:T(8,128)(2,1)S(1)} fusion(bf16[512,16,256]{2,1,0:T(8,128)(2,1)} %param.5, bf16[512,256]{1,0:T(8,128)(2,1)S(1)} %bitcast.21), kind=kLoop, calls=%fused_computation.6 | loop fusion | flops 2097152 | bytes 8650752 | tf_op jit(solution)/shard_map/mul | solution.py:20
  11.5 1.9 %copy-done.2 = bf16[1024,16,256]{2,1,0:T(8,128)(2,1)S(1)} copy-done((bf16[1024,16,256]{2,1,0:T(8,128)(2,1)S(1)}, bf16[1024,16,256]{2,1,0:T(8,128)(2,1)}, u32[]{:S(2)}) %copy-start.2) | copy-done | bytes 8388632
  13.4 9.2 %fusion.3 = f32[512,1024]{1,0:T(8,128)} fusion(bf16[1024,16,256]{2,1,0:T(8,128)(2,1)S(1)} %copy-done.2, bf16[512,16,256]{2,1,0:T(8,128)(2,1)S(1)} %broadcast_multiply_fusion), kind=kOutput, calls=%fused_computation.7 | convolution fusion | flops 4294967296 | bytes 14680064 | tf_op jit(solution)/shard_map/pcd,rcd->pr/dot_general | solution.py:21
  22.7 0.1 dynamic-slice_xor_fusion
  22.7 4.4 %select_reduce_fusion = s32[512]{0:T(512)S(1)} fusion(s32[16384]{0:T(1024)S(1)} %add_select_fusion, s32[16384]{0:T(1024)S(1)} %copy-done.1, s32[512]{0:T(512)S(1)} %get-tuple-element.7), kind=kLoop, calls=%fused_computation.2 | loop fusion | flops 25165312 | bytes 135168 | tf_op jit(solution)/shard_map/reduce_sum | solution.py:30
  27.2 0.3 convert_reduce_fusion
  27.5 0.2 select_reduce_fusion.1
  27.8 33.8 %reduce-scatter.2.cloned.1.call-done = f32[512,128]{1,0:T(8,128)} async-done(((f32[512,1024]{1,0:T(8,128)}), f32[512,128]{1,0:T(8,128)}) %reduce-scatter.2.cloned.1.call-update) | async-done | bytes 262160 | tf_op jit(solution)/shard_map/reduce_scatter | solution.py:25
  61.6 1.1 copy.26
  62.7 0.7 copy.27
  63.5 3.4 %all-to-all-start = ((f32[512,4,8,4]{0,3,1,2:T(4,128)}), f32[512,4,8,4]{0,3,1,2:T(4,128)S(1)}, u32[]{:S(2)}, u32[]{:S(2)}) async-start(f32[512,4,8,4]{0,3,1,2:T(4,128)} %copy.27), calls=%async_computation.1 | async-start | bytes 524288 | tf_op jit(solution)/shard_map/all_to_all | solution.py:38
  66.9 0.1 reduce_sum.34
  67.0 7.3 %all-to-all-done = f32[512,4,8,4]{0,3,1,2:T(4,128)S(1)} async-done(((f32[512,4,8,4]{0,3,1,2:T(4,128)}), f32[512,4,8,4]{0,3,1,2:T(4,128)S(1)}, u32[]{:S(2)}, u32[]{:S(2)}) %all-to-all-start) | async-done | bytes 262176 | tf_op jit(solution)/shard_map/all_to_all | solution.py:38
  74.3 0.1 copy.28
  74.4 0.1 copy.29
  74.6 1.6 %gather_fusion = f32[544,128]{1,0:T(8,128)S(1)} fusion(f32[512,128]{1,0:T(8,128)S(1)} %copy.29, s32[1024]{0:T(1024)S(1)} %pad_clamp_fusion.1), kind=kCustom, calls=%fused_computation | custom fusion | bytes 559232 | tf_op jit(solution)/shard_map/jit(_take)/gather | solution.py:44
  76.2 0.9 broadcast_select_fusion
  77.1 10.1 %all-to-all-start.1 = ((f32[32,17,128]{2,1,0:T(8,128)}), f32[32,17,128]{2,1,0:T(8,128)S(1)}, u32[]{:S(2)}, u32[]{:S(2)}) async-start(f32[32,17,128]{2,1,0:T(8,128)} %broadcast_select_fusion), calls=%async_computation.2 | async-start | bytes 786432 | tf_op jit(solution)/shard_map/all_to_all | solution.py:45
  87.2 14.6 %all-to-all-done.1 = f32[32,17,128]{2,1,0:T(8,128)S(1)} async-done(((f32[32,17,128]{2,1,0:T(8,128)}), f32[32,17,128]{2,1,0:T(8,128)S(1)}, u32[]{:S(2)}, u32[]{:S(2)}) %all-to-all-start.1) | async-done | bytes 278560 | tf_op jit(solution)/shard_map/all_to_all | solution.py:45
  101.8 1.0 gather_fusion.1
  102.9 0.8 select_add_fusion
  (18 shorter events, 0.3 us)
Async XLA Ops:
  6.5 55.0 %reduce-scatter.2.cloned.1.call-start = ((), (), s32[]{:S(2)}) async-start(), calls=%async_computation.3 | async-start | bytes 2359296 | tf_op jit(solution)/shard_map/reduce_scatter | solution.py:25
  8.8 4.6 %copy-start.2 = (bf16[1024,16,256]{2,1,0:T(8,128)(2,1)S(1)}, bf16[1024,16,256]{2,1,0:T(8,128)(2,1)}, u32[]{:S(2)}) copy-start(bf16[1024,16,256]{2,1,0:T(8,128)(2,1)} %param.6) | copy-start | bytes 25165828
  13.4 9.2 %copy-start.1 = (s32[16384]{0:T(1024)S(1)}, s32[16384]{0:T(1024)}, u32[]{:S(2)}) copy-start(s32[16384]{0:T(1024)} %param.9) | copy-start | bytes 196612
  63.5 10.9 %all-to-all-start = ((f32[512,4,8,4]{0,3,1,2:T(4,128)}), f32[512,4,8,4]{0,3,1,2:T(4,128)S(1)}, u32[]{:S(2)}, u32[]{:S(2)}) async-start(f32[512,4,8,4]{0,3,1,2:T(4,128)} %copy.27), calls=%async_computation.1 | async-start | bytes 524288 | tf_op jit(solution)/shard_map/all_to_all | solution.py:38
  74.4 28.5 %copy-start = (f32[512,128]{1,0:T(8,128)S(1)}, f32[512,128]{1,0:T(8,128)}, u32[]{:S(2)}) copy-start(f32[512,128]{1,0:T(8,128)} %reduce-scatter.2.cloned.1.call-done) | copy-start | bytes 786436
  77.1 24.7 %all-to-all-start.1 = ((f32[32,17,128]{2,1,0:T(8,128)}), f32[32,17,128]{2,1,0:T(8,128)S(1)}, u32[]{:S(2)}, u32[]{:S(2)}) async-start(f32[32,17,128]{2,1,0:T(8,128)} %broadcast_select_fusion), calls=%async_computation.2 | async-start | bytes 786432 | tf_op jit(solution)/shard_map/all_to_all | solution.py:45
Sparse Core Ops, SparseCore 0:
  22.8 38.7 reduce-scatter.1

commit v2 on v0

v2 whole, which is shorter than its diff:
```python
import functools

import jax
import jax.numpy as jnp
from jax import lax
from jax.experimental import pallas as pl
from jax.experimental.pallas import tpu as pltpu
from jax.sharding import PartitionSpec as P

MESH = pl.DeviceIdType.MESH
F32 = jnp.float32
BF16 = jnp.bfloat16
NX = 4
CORES = 2
VIRT = NX * CORES
BLOCK = 128
STEPS = (2, 1, 3, 0)
NT = (((1,), (1,)), ((), ()))
NN = (((1,), (0,)), ((), ()))


def split_two(value):
    high = value.astype(BF16)
    return high, (value - high.astype(F32)).astype(BF16)


def iota(shape, dim):
    return lax.broadcasted_iota(jnp.int32, shape, dim)


def flatten_into(dst, row, block, cs, width):
    flat = pltpu.einshape("pcd->p(cd)", block)
    for j in range(2):
        for c in range(cs):
            at = j * cs * 128 + c * 128
            dst[pl.ds(row, 16), at:at + 128] = flat[:, c * width + j * 128:c * width + (j + 1) * 128]


def kernel(
    n_pair, slots,
    amp, ints, mask_ref, slab_ref, owner_ref, out_ref,
    amp_raw, amp_flat, int_raw, int_flat, part, chip_in, acc, fwd, fin_left, fin_right,
    turned, sent, came, send_one, take_one,
    amp_sem, int_sem, chip_send, chip_recv, ring_send, ring_recv, turn_send, turn_recv, pair_send, pair_recv,
):
    rows, cs, width = amp_raw.shape
    tiles = rows // 128
    half_k = cs * 128
    half = BLOCK // 2
    me_p = lax.axis_index("pair")
    me_v = lax.axis_index("virt")
    x = me_v // CORES
    core = me_v % CORES
    other = me_v + 1 - 2 * core
    right = ((x + 1) % NX) * CORES + core
    left = ((x + NX - 1) % NX) * CORES + core

    def fetch_amp(q):
        at = pl.ds(q * 128, 128)
        return pltpu.make_async_copy(amp.at[at], amp_raw.at[at], amp_sem.at[q])

    def fetch_ints(k):
        to = (x + STEPS[k]) % NX
        at = pl.ds(pl.multiple_of(to * CORES * BLOCK, CORES * BLOCK), CORES * BLOCK)
        return pltpu.make_async_copy(ints.at[at], int_raw.at[k], int_sem.at[k])

    for q in range(tiles):
        fetch_amp(q).start()
    for k in range(NX):
        fetch_ints(k).start()

    barrier = pltpu.get_barrier_semaphore()

    @pl.loop(1, VIRT)
    def _(i):
        pl.semaphore_signal(barrier, inc=1, device_id=(me_p, (me_v + i) % VIRT), device_id_type=MESH)

    @pl.loop(1, n_pair)
    def _(i):
        pl.semaphore_signal(barrier, inc=1, device_id=((me_p + i) % n_pair, me_v), device_id_type=MESH)

    for q in range(tiles):
        fetch_amp(q).wait()

        @pl.loop(0, 8, unroll=4)
        def _(g):
            row = pl.multiple_of(q * 128 + g * 16, 16)
            flatten_into(amp_flat, row, amp_raw[pl.ds(row, 16)], cs, width)

    select = mask_ref[slab_ref[0] // 8].astype(F32)

    def multiply(k):
        fetch_ints(k).wait()
        flat = int_flat.at[k % 2]

        @pl.loop(0, CORES * VIRT, unroll=4)
        def _(g):
            base = (g // VIRT) * BLOCK + 4 * (g % VIRT)
            block = jnp.concatenate([int_raw[k, pl.ds(base + 32 * a, 4)] for a in range(4)], axis=0)
            flatten_into(flat, pl.multiple_of(g * 16, 16), block, cs, width)

        for nb in range(rows // 128 // 2 if rows > 128 else 1):
            ps = slice(nb * 256, nb * 256 + 256) if rows > 128 else slice(0, 128)
            one = lax.dot_general(flat[:, :half_k], amp_flat[ps, :half_k], NT, preferred_element_type=F32)
            two = lax.dot_general(flat[:, half_k:], amp_flat[ps, half_k:], NT, preferred_element_type=F32)
            value = one * select[0:1, ps] + two * select[1:2, ps]
            for c in range(CORES):
                part[k, c, :, ps] = value[c * BLOCK:(c + 1) * BLOCK]

    def chip_copy(k):
        return pltpu.make_async_remote_copy(
            src_ref=part.at[k, 1 - core], dst_ref=chip_in.at[k], send_sem=chip_send.at[k], recv_sem=chip_recv.at[k],
            device_id=(me_p, other), device_id_type=MESH)

    def ring_copy(i, src, dst, to):
        return pltpu.make_async_remote_copy(
            src_ref=src, dst_ref=dst, send_sem=ring_send.at[i], recv_sem=ring_recv.at[i],
            device_id=(me_p, to), device_id_type=MESH)

    low, high = pl.ds(0, half), pl.ds(half, half)
    ring = [
        ring_copy(0, acc.at[0, low], fwd.at[0], right),
        ring_copy(1, acc.at[0, high], fwd.at[1], left),
        ring_copy(2, acc.at[1, high], fin_left.at[high], right),
        ring_copy(3, acc.at[1, low], fin_left.at[low], right),
        ring_copy(4, acc.at[2, low], fin_right.at[low], left),
        ring_copy(5, acc.at[2, high], fin_right.at[high], left),
    ]

    def chip_sum(k):
        chip_copy(k).wait_recv()
        acc[k] = part[k, core] + chip_in[k]

    multiply(0)
    pl.semaphore_wait(barrier, VIRT - 1 + n_pair - 1)
    chip_copy(0).start()
    multiply(1)
    chip_copy(1).start()
    chip_sum(0)
    ring[0].start()
    ring[1].start()
    multiply(2)
    chip_copy(2).start()
    chip_sum(1)
    ring[2].start()
    ring[0].wait_recv()
    acc[1, low] += fwd[0]
    ring[3].start()
    multiply(3)
    chip_copy(3).start()
    chip_sum(2)
    ring[4].start()
    ring[1].wait_recv()
    acc[2, high] += fwd[1]
    ring[5].start()

    eye = iota((128, 128), 0) == iota((128, 128), 1)

    def as_column(row):
        return jnp.sum(jnp.where(eye, row, 0.0), axis=1, keepdims=True)

    def as_row(column):
        return jnp.sum(jnp.where(eye, column, 0.0), axis=0, keepdims=True)

    own_rows = [owner_ref[pl.ds(me_p * tiles + t, 1), :] for t in range(tiles)]
    wanted = [as_column((r ^ 1).astype(F32)).astype(jnp.int32) for r in own_rows]
    order_rows = [(r // 2).astype(F32) for r in own_rows]
    order_columns = [as_column(r) for r in order_rows]
    there_columns = []
    for t in range(tiles):
        want = jnp.broadcast_to(wanted[t], (128, 128))

        def look(g, found):
            return jnp.where(owner_ref[pl.ds(g, 1), :] == want, g // tiles, found)

        found = lax.fori_loop(0, n_pair * tiles, look, jnp.zeros((128, 128), jnp.int32), unroll=4)
        there_columns.append(jnp.max(found.astype(F32), axis=1, keepdims=True))
    there_rows = [as_row(c) for c in there_columns]
    places = []
    for t in range(tiles):
        before = jnp.zeros((128, 128), F32)
        for u in range(tiles):
            hit = (there_rows[u] == there_columns[t]) & (order_rows[u] < order_columns[t])
            before = before + jnp.where(hit, 1.0, 0.0)
        places.append(there_columns[t] * slots + jnp.sum(before, axis=1, keepdims=True))
    n_slots = n_pair * slots
    for t in range(tiles):
        at = slice(t * 128, (t + 1) * 128)
        column = places[t].astype(jnp.int32)
        take_one[at, :] = jnp.where(iota((128, n_slots), 1) == column, 1.0, 0.0).astype(BF16)
        row = as_row(places[t]).astype(jnp.int32)
        send_one[:, at] = jnp.where(iota((n_slots, 128), 0) == row, 1.0, 0.0).astype(BF16)

    chip_sum(3)
    for i in range(2, 6):
        ring[i].wait_recv()
    acc[3] = acc[3] + fin_left[...] + fin_right[...]

    def turn_copy(i):
        to = (me_v + i) % VIRT
        src = acc.at[3, pl.ds(pl.multiple_of(to * 16, 16), 16)]
        dst = turned.at[pl.ds(pl.multiple_of(me_v * 16, 16), 16)]
        return pltpu.make_async_remote_copy(
            src_ref=src, dst_ref=dst, send_sem=turn_send.at[i], recv_sem=turn_recv.at[i],
            device_id=(me_p, to), device_id_type=MESH)

    for i in range(1, VIRT):
        turn_copy(i).start()
    mine = pl.ds(pl.multiple_of(me_v * 16, 16), 16)
    turned[mine, :] = acc[3, mine, :]
    came[pl.ds(me_p, 1)] = jnp.zeros((1, slots, BLOCK), F32)

    own_high, own_low = split_two(acc[3])
    diagonal = jnp.where(iota((rows, rows), 0) == iota((rows, rows), 1), 1.0, 0.0).astype(BF16)
    own_pair = lax.dot_general(diagonal, jnp.concatenate([own_high, own_low], axis=0), NT, preferred_element_type=F32)
    source, target = iota((BLOCK, BLOCK), 0), iota((BLOCK, BLOCK), 1)
    group, first, second = source // 16, (source // 4) % 4, source % 4
    own_lanes = jnp.where(target == first * 32 + group * 4 + second, 1.0, 0.0).astype(BF16)
    mirror_lanes = jnp.where(target == second * 32 + group * 4 + first, 1.0, 0.0).astype(BF16)
    own_lanes = jnp.concatenate([own_lanes, own_lanes], axis=0)
    mirror_lanes = jnp.concatenate([mirror_lanes, mirror_lanes], axis=0)
    out_ref[...] = lax.dot_general(own_pair.astype(BF16), own_lanes, NN, preferred_element_type=F32)

    for i in range(1, VIRT):
        turn_copy(i).wait_recv()
    turned_high, turned_low = split_two(turned[...])
    both = lax.dot_general(
        send_one[...], jnp.concatenate([turned_high, turned_low], axis=0), NT, preferred_element_type=F32)
    sent[...] = (both[:, :BLOCK] + both[:, BLOCK:]).reshape(n_pair, slots, BLOCK)

    def pair_copy(i):
        to = (me_p + i) % n_pair
        return pltpu.make_async_remote_copy(
            src_ref=sent.at[to], dst_ref=came.at[me_p], send_sem=pair_send.at[i], recv_sem=pair_recv.at[i],
            device_id=(to, me_v), device_id_type=MESH)

    @pl.loop(1, n_pair)
    def _(i):
        pair_copy(i).start()

    @pl.loop(1, n_pair)
    def _(i):
        pair_copy(i).wait_recv()

    came_high, came_low = split_two(came[...].reshape(n_slots, BLOCK))
    fetched = lax.dot_general(
        take_one[...], jnp.concatenate([came_high, came_low], axis=1), NN, preferred_element_type=F32)
    out_ref[...] += lax.dot_general(fetched.astype(BF16), mirror_lanes, NN, preferred_element_type=F32)

    for k in range(NX):
        chip_copy(k).wait_send()
    for copy in ring:
        copy.wait_send()
    for i in range(1, VIRT):
        turn_copy(i).wait_send()

    @pl.loop(1, n_pair)
    def _(i):
        pair_copy(i).wait_send()


def per_device(n_pair, slots, amplitudes, integrals, mask, slab, owner):
    rows, cs, width = amplitudes.shape
    dma = pltpu.SemaphoreType.DMA
    n_slots = n_pair * slots
    half = BLOCK // 2
    return pl.pallas_call(
        functools.partial(kernel, n_pair, slots),
        out_shape=jax.ShapeDtypeStruct((rows, BLOCK), F32),
        in_specs=[
            pl.BlockSpec(memory_space=pl.ANY),
            pl.BlockSpec(memory_space=pl.ANY),
            pl.BlockSpec(memory_space=pltpu.VMEM),
            pl.BlockSpec(memory_space=pltpu.SMEM),
            pl.BlockSpec(memory_space=pltpu.VMEM),
        ],
        out_specs=pl.BlockSpec(memory_space=pltpu.VMEM),
        scratch_shapes=[
            pltpu.VMEM((rows, cs, width), BF16),
            pltpu.VMEM((rows, cs * width), BF16),
            pltpu.VMEM((NX, CORES * BLOCK, cs, width), BF16),
            pltpu.VMEM((2, CORES * BLOCK, cs * width), BF16),
            pltpu.VMEM((NX, CORES, BLOCK, rows), F32),
            pltpu.VMEM((NX, BLOCK, rows), F32),
            pltpu.VMEM((NX, BLOCK, rows), F32),
            pltpu.VMEM((2, half, rows), F32),
            pltpu.VMEM((BLOCK, rows), F32),
            pltpu.VMEM((BLOCK, rows), F32),
            pltpu.VMEM((BLOCK, rows), F32),
            pltpu.VMEM((n_pair, slots, BLOCK), F32),
            pltpu.VMEM((n_pair, slots, BLOCK), F32),
            pltpu.VMEM((n_slots, rows), BF16),
            pltpu.VMEM((rows, n_slots), BF16),
            dma((rows // 128,)),
            dma((NX,)),
            dma((NX,)),
            dma((NX,)),
            dma((6,)),
            dma((6,)),
            dma((VIRT,)),
            dma((VIRT,)),
            dma((n_pair,)),
            dma((n_pair,)),
        ],
        compiler_params=pltpu.CompilerParams(
            collective_id=0, has_side_effects=True, vmem_limit_bytes=56 * 2**20),
        cost_estimate=pl.CostEstimate(
            flops=2 * rows * cs * width * VIRT * BLOCK, bytes_accessed=13 * 2**20, transcendentals=0),
    )(amplitudes, integrals, jnp.transpose(mask, (1, 2, 0)), slab, owner.reshape(-1, 128))


def solution(mesh, slots=24):
    return jax.shard_map(
        functools.partial(per_device, mesh.shape["pair"], slots),
        mesh=mesh,
        in_specs=(
            P("pair", None, "virt"),
            P(None, None, "virt"),
            P("pair", None, "virt"),
            P(),
            P(),
        ),
        out_specs=P("pair", "virt"),
        check_vma=False,
    )
```

time: 186 us -> 52.3 us (0.28)
  waiting for transfers between devices: 131 us -> 0 us
  Pallas kernels: 0 us -> 49.3 us
  between operations: 14.2 us -> 0.66 us
  blocking collectives: 12.2 us -> 0 us
  other arithmetic: 10.3 us -> 0 us
  matrix products: 9.21 us -> 0 us
  local copies, waits for them, and re-layouts: 8.48 us -> 1.67 us
    all_gather x1 -> x0, waiting for transfers between devices: 93.3 us -> none  [per_device(): gathered = lax.all_gather(swapped, 'pair', axis=0, tiled=True)]
    pallas_call x0 -> x1, Pallas kernels: none -> 49.3 us  [per_device(): pl.pallas_call(functools.partial(kernel, n_pair, slots), out_shape=jax.Sh...]
    reduce_scatter x1 -> x0, waiting for transfers between devices: 37.4 us -> none  [per_device(): lax.psum_scatter(partial_value, 'virt', scatter_dimension=1, tiled=True)]
    all_to_all x1 -> x0, blocking collectives: 12.2 us -> none  [per_device(): lax.all_to_all(blocks, 'virt', split_axis=2, concat_axis=1, tiled=True)]
    dot_general x1 -> x0, matrix products: 9.21 us -> none  [per_device(): jnp.einsum('pcd,rcd->pr', masked, integrals, preferred_element_type=jnp.f...]
    reduce_sum x2 -> x0, other arithmetic: 5.59 us -> none  [the longest x1 4.65 us: per_device(): mirror_slots = jnp.sum(jnp.where(matches, slot_ids[None, :], 0), axis=1)]
    gather x1 -> x0, local copies, waits for them, and re-layouts: 4.41 us -> none  [per_device(): fetched = jnp.take(gathered, mirror_slots, axis=0)]
    mul x1 -> x0, other arithmetic: 2.83 us -> none  [per_device(): tiled * picked_soft[:, None, :, None]]
  transfers between devices with their start and end apart: 2 -> 0, of which waited for: 2 -> 0; matrix products, arithmetic and copies ran while one was open for 3% -> 0% of each run, Pallas kernels for 0% -> 0%
where the time goes in v2:
time: 52.3 us; the launch traced here: 51.7 us
  Pallas kernels  49.3 us (94%)
  local copies, waits for them, and re-layouts  1.67 us (3%)
  between operations  0.66 us (1%)
    pallas_call x1, Pallas kernels, per_device(): pl.pallas_call(functools.partial(kernel, n_pair, slots), out_shape=jax.Sh...  49.3 us
    unnamed x1, local copies, waits for them, and re-layouts  1.67 us

profile of v2, /device:TPU:1, one launch (start us, length us, event | category | flops | bytes accessed | tf_op | source)
XLA Modules:
  0.0 51.7 jit_solution(779440397023776902)
XLA Ops:
  0.7 49.3 %shard_map.55 = f32[512,128]{1,0:T(8,128)} custom-call(bf16[512,16,256]{2,1,0:T(8,128)(2,1)} %amp.1, bf16[1024,16,256]{2,1,0:T(8,128)(2,1)} %ints.1, s32[16,2,512]{2,1,0:T(2,128)} %bitcast.2, s32[1]{0:T(128)S(6)} %copy.7.slab_ref, s32[128,128]{1,0:T(8,128)} %bitcast.3), custom_call_target="tpu_custom_call" | custom-call | flops 4294967296 | bytes 13631488 | tf_op jit(solution)/shard_map/pallas_call | solution.py:267
  50.0 1.7 %copy.8 = f32[512,128]{1,0:T(8,128)} copy(f32[512,128]{1,0:T(8,128)} %shard_map.55) | data formatting | bytes 524288

commit v3 on v2

--- a/solution.py
+++ b/solution.py
@@ -14,7 +14,7 @@
 CORES = 2
 VIRT = NX * CORES
 BLOCK = 128
-STEPS = (2, 1, 3, 0)
+PAD = 24
 NT = (((1,), (1,)), ((), ()))
 NN = (((1,), (0,)), ((), ()))
 
@@ -38,7 +38,7 @@
 
 def kernel(
     n_pair, slots,
-    amp, ints, mask_ref, slab_ref, owner_ref, out_ref,
+    amp, ints, mask_ref, slab_ref, owner_ref, own_ref, fetched_ref,
     amp_raw, amp_flat, int_raw, int_flat, part, chip_in, acc, fwd, fin_left, fin_right,
     turned, sent, came, send_one, take_one,
     amp_sem, int_sem, chip_send, chip_recv, ring_send, ring_recv, turn_send, turn_recv, pair_send, pair_recv,
@@ -59,15 +59,13 @@
         at = pl.ds(q * 128, 128)
         return pltpu.make_async_copy(amp.at[at], amp_raw.at[at], amp_sem.at[q])
 
-    def fetch_ints(k):
-        to = (x + STEPS[k]) % NX
-        at = pl.ds(pl.multiple_of(to * CORES * BLOCK, CORES * BLOCK), CORES * BLOCK)
-        return pltpu.make_async_copy(ints.at[at], int_raw.at[k], int_sem.at[k])
+    def fetch_ints(s):
+        to = (x + (2, 1, 3, 0)[s]) % NX
+        return pltpu.make_async_copy(ints.at[:, pl.ds(to * CORES * 4, CORES * 4)], int_raw.at[s], int_sem.at[s])
 
     for q in range(tiles):
         fetch_amp(q).start()
-    for k in range(NX):
-        fetch_ints(k).start()
+    fetch_ints(0).start()
 
     barrier = pltpu.get_barrier_semaphore()
 
@@ -87,25 +85,35 @@
             row = pl.multiple_of(q * 128 + g * 16, 16)
             flatten_into(amp_flat, row, amp_raw[pl.ds(row, 16)], cs, width)
 
+    for s in range(1, NX):
+        fetch_ints(s).start()
     select = mask_ref[slab_ref[0] // 8].astype(F32)
-
-    def multiply(k):
-        fetch_ints(k).wait()
+    runs = (((0, 0), (0, 4)), ((1, 4), (2, 0)), ((1, 0), (2, 4)), ((3, 0), (3, 4)))
+
+    def arrange(k):
         flat = int_flat.at[k % 2]
-
-        @pl.loop(0, CORES * VIRT, unroll=4)
-        def _(g):
-            base = (g // VIRT) * BLOCK + 4 * (g % VIRT)
-            block = jnp.concatenate([int_raw[k, pl.ds(base + 32 * a, 4)] for a in range(4)], axis=0)
-            flatten_into(flat, pl.multiple_of(g * 16, 16), block, cs, width)
-
-        for nb in range(rows // 128 // 2 if rows > 128 else 1):
-            ps = slice(nb * 256, nb * 256 + 256) if rows > 128 else slice(0, 128)
-            one = lax.dot_general(flat[:, :half_k], amp_flat[ps, :half_k], NT, preferred_element_type=F32)
-            two = lax.dot_general(flat[:, half_k:], amp_flat[ps, half_k:], NT, preferred_element_type=F32)
-            value = one * select[0:1, ps] + two * select[1:2, ps]
-            for c in range(CORES):
-                part[k, c, :, ps] = value[c * BLOCK:(c + 1) * BLOCK]
+        for c in range(CORES):
+            for r in range(2):
+                s, first = runs[k][r]
+
+                @pl.loop(0, 4, unroll=4)
+                def _(g):
+                    block = jnp.concatenate(
+                        [int_raw[s, (first + g) * 4 + a, pl.ds(c * 4, 4)] for a in range(4)], axis=0)
+                    row = pl.multiple_of((c * 8 + r * 4 + g) * 16, 16)
+                    flatten_into(flat, row, block, cs, width)
+
+    def multiply(k, nb):
+        flat = int_flat.at[k % 2]
+        span = min(256, rows)
+        ps = slice(nb * span, (nb + 1) * span)
+        one = lax.dot_general(flat[:, :half_k], amp_flat[ps, :half_k], NT, preferred_element_type=F32)
+        two = lax.dot_general(flat[:, half_k:], amp_flat[ps, half_k:], NT, preferred_element_type=F32)
+        value = one * select[0:1, ps] + two * select[1:2, ps]
+        for c in range(CORES):
+            part[k, c, :, ps] = value[c * BLOCK:(c + 1) * BLOCK]
+
+    later = range(1, rows // min(256, rows))
 
     def chip_copy(k):
         return pltpu.make_async_remote_copy(
@@ -121,9 +129,9 @@
     ring = [
         ring_copy(0, acc.at[0, low], fwd.at[0], right),
         ring_copy(1, acc.at[0, high], fwd.at[1], left),
-        ring_copy(2, acc.at[1, high], fin_left.at[high], right),
-        ring_copy(3, acc.at[1, low], fin_left.at[low], right),
-        ring_copy(4, acc.at[2, low], fin_right.at[low], left),
+        ring_copy(2, acc.at[1, low], fin_left.at[high], right),
+        ring_copy(3, acc.at[1, high], fin_right.at[low], left),
+        ring_copy(4, acc.at[2, low], fin_left.at[low], right),
         ring_copy(5, acc.at[2, high], fin_right.at[high], left),
     ]
 
@@ -131,24 +139,40 @@
         chip_copy(k).wait_recv()
         acc[k] = part[k, core] + chip_in[k]
 
-    multiply(0)
+    fetch_ints(0).wait()
+    arrange(0)
+    multiply(0, 0)
+    for nb in later:
+        multiply(0, nb)
     pl.semaphore_wait(barrier, VIRT - 1 + n_pair - 1)
     chip_copy(0).start()
-    multiply(1)
-    chip_copy(1).start()
+    fetch_ints(1).wait()
+    fetch_ints(2).wait()
+    arrange(1)
+    multiply(1, 0)
     chip_sum(0)
     ring[0].start()
     ring[1].start()
-    multiply(2)
-    chip_copy(2).start()
+    for nb in later:
+        multiply(1, nb)
+    chip_copy(1).start()
+    arrange(2)
+    multiply(2, 0)
     chip_sum(1)
     ring[2].start()
+    ring[3].start()
+    for nb in later:
+        multiply(2, nb)
+    chip_copy(2).start()
+    fetch_ints(3).wait()
+    arrange(3)
+    multiply(3, 0)
+    chip_sum(2)
+    for nb in later:
+        multiply(3, nb)
+    chip_copy(3).start()
     ring[0].wait_recv()
-    acc[1, low] += fwd[0]
-    ring[3].start()
-    multiply(3)
-    chip_copy(3).start()
-    chip_sum(2)
+    acc[2, low] += fwd[0]
     ring[4].start()
     ring[1].wait_recv()
     acc[2, high] += fwd[1]
@@ -182,8 +206,8 @@
         for u in range(tiles):
             hit = (there_rows[u] == there_columns[t]) & (order_rows[u] < order_columns[t])
             before = before + jnp.where(hit, 1.0, 0.0)
-        places.append(there_columns[t] * slots + jnp.sum(before, axis=1, keepdims=True))
-    n_slots = n_pair * slots
+        places.append(there_columns[t] * PAD + jnp.sum(before, axis=1, keepdims=True))
+    n_slots = n_pair * PAD
     for t in range(tiles):
         at = slice(t * 128, (t + 1) * 128)
         column = places[t].astype(jnp.int32)
@@ -191,10 +215,33 @@
         row = as_row(places[t]).astype(jnp.int32)
         send_one[:, at] = jnp.where(iota((n_slots, 128), 0) == row, 1.0, 0.0).astype(BF16)
 
+    came[pl.ds(me_p, 1)] = jnp.zeros((1, slots, BLOCK), F32)
+    source, target = iota((BLOCK, BLOCK), 0), iota((BLOCK, BLOCK), 1)
+    group, first, second = source // 16, (source // 4) % 4, source % 4
+    own_lanes = jnp.where(target == first * 32 + group * 4 + second, 1.0, 0.0).astype(BF16)
+    mirror_lanes = jnp.where(target == second * 32 + group * 4 + first, 1.0, 0.0).astype(BF16)
+    own_lanes = jnp.concatenate([own_lanes, own_lanes], axis=0)
+    mirror_lanes = jnp.concatenate([mirror_lanes, mirror_lanes], axis=0)
+    diagonal = jnp.where(iota((rows, rows), 0) == iota((rows, rows), 1), 1.0, 0.0).astype(BF16)
+
     chip_sum(3)
     for i in range(2, 6):
         ring[i].wait_recv()
     acc[3] = acc[3] + fin_left[...] + fin_right[...]
+    sum_high, sum_low = split_two(acc[3])
+    both = lax.dot_general(
+        send_one[...], jnp.concatenate([sum_high, sum_low], axis=0), NT, preferred_element_type=F32)
+    sent[...] = (both[:, :BLOCK] + both[:, BLOCK:]).reshape(n_pair, PAD, BLOCK)[:, :slots]
+
+    def pair_copy(i):
+        to = (me_p + i) % n_pair
+        return pltpu.make_async_remote_copy(
+            src_ref=sent.at[to], dst_ref=came.at[me_p], send_sem=pair_send.at[i], recv_sem=pair_recv.at[i],
+            device_id=(to, me_v), device_id_type=MESH)
+
+    @pl.loop(1, n_pair)
+    def _(i):
+        pair_copy(i).start()
 
     def turn_copy(i):
         to = (me_v + i) % VIRT
@@ -208,44 +255,21 @@
         turn_copy(i).start()
     mine = pl.ds(pl.multiple_of(me_v * 16, 16), 16)
     turned[mine, :] = acc[3, mine, :]
-    came[pl.ds(me_p, 1)] = jnp.zeros((1, slots, BLOCK), F32)
-
-    own_high, own_low = split_two(acc[3])
-    diagonal = jnp.where(iota((rows, rows), 0) == iota((rows, rows), 1), 1.0, 0.0).astype(BF16)
-    own_pair = lax.dot_general(diagonal, jnp.concatenate([own_high, own_low], axis=0), NT, preferred_element_type=F32)
-    source, target = iota((BLOCK, BLOCK), 0), iota((BLOCK, BLOCK), 1)
-    group, first, second = source // 16, (source // 4) % 4, source % 4
-    own_lanes = jnp.where(target == first * 32 + group * 4 + second, 1.0, 0.0).astype(BF16)
-    mirror_lanes = jnp.where(target == second * 32 + group * 4 + first, 1.0, 0.0).astype(BF16)
-    own_lanes = jnp.concatenate([own_lanes, own_lanes], axis=0)
-    mirror_lanes = jnp.concatenate([mirror_lanes, mirror_lanes], axis=0)
-    out_ref[...] = lax.dot_general(own_pair.astype(BF16), own_lanes, NN, preferred_element_type=F32)
-
     for i in range(1, VIRT):
         turn_copy(i).wait_recv()
-    turned_high, turned_low = split_two(turned[...])
-    both = lax.dot_general(
-        send_one[...], jnp.concatenate([turned_high, turned_low], axis=0), NT, preferred_element_type=F32)
-    sent[...] = (both[:, :BLOCK] + both[:, BLOCK:]).reshape(n_pair, slots, BLOCK)
-
-    def pair_copy(i):
-        to = (me_p + i) % n_pair
-        return pltpu.make_async_remote_copy(
-            src_ref=sent.at[to], dst_ref=came.at[me_p], send_sem=pair_send.at[i], recv_sem=pair_recv.at[i],
-            device_id=(to, me_v), device_id_type=MESH)
+    own_high, own_low = split_two(turned[...])
+    own_pair = lax.dot_general(diagonal, jnp.concatenate([own_high, own_low], axis=0), NT, preferred_element_type=F32)
+    own_ref[...] = lax.dot_general(own_pair.astype(BF16), own_lanes, NN, preferred_element_type=F32)
 
     @pl.loop(1, n_pair)
     def _(i):
-        pair_copy(i).start()
-
-    @pl.loop(1, n_pair)
-    def _(i):
         pair_copy(i).wait_recv()
 
-    came_high, came_low = split_two(came[...].reshape(n_slots, BLOCK))
+    rest = jnp.zeros((n_pair, PAD - slots, BLOCK), F32)
+    came_high, came_low = split_two(jnp.concatenate([came[...], rest], axis=1).reshape(n_slots, BLOCK))
     fetched = lax.dot_general(
         take_one[...], jnp.concatenate([came_high, came_low], axis=1), NN, preferred_element_type=F32)
-    out_ref[...] += lax.dot_general(fetched.astype(BF16), mirror_lanes, NN, preferred_element_type=F32)
+    fetched_ref[...] = lax.dot_general(fetched.astype(BF16), mirror_lanes, NN, preferred_element_type=F32)
 
     for k in range(NX):
         chip_copy(k).wait_send()
@@ -262,11 +286,11 @@
 def per_device(n_pair, slots, amplitudes, integrals, mask, slab, owner):
     rows, cs, width = amplitudes.shape
     dma = pltpu.SemaphoreType.DMA
-    n_slots = n_pair * slots
+    n_slots = n_pair * PAD
     half = BLOCK // 2
-    return pl.pallas_call(
+    own, fetched = pl.pallas_call(
         functools.partial(kernel, n_pair, slots),
-        out_shape=jax.ShapeDtypeStruct((rows, BLOCK), F32),
+        out_shape=[jax.ShapeDtypeStruct((rows, BLOCK), F32)] * 2,
         in_specs=[
             pl.BlockSpec(memory_space=pl.ANY),
             pl.BlockSpec(memory_space=pl.ANY),
@@ -274,11 +298,11 @@
             pl.BlockSpec(memory_space=pltpu.SMEM),
             pl.BlockSpec(memory_space=pltpu.VMEM),
         ],
-        out_specs=pl.BlockSpec(memory_space=pltpu.VMEM),
+        out_specs=[pl.BlockSpec(memory_space=pltpu.VMEM)] * 2,
         scratch_shapes=[
             pltpu.VMEM((rows, cs, width), BF16),
             pltpu.VMEM((rows, cs * width), BF16),
-            pltpu.VMEM((NX, CORES * BLOCK, cs, width), BF16),
+            pltpu.VMEM((NX, 32, CORES * 4, cs, width), BF16),
             pltpu.VMEM((2, CORES * BLOCK, cs * width), BF16),
             pltpu.VMEM((NX, CORES, BLOCK, rows), F32),
             pltpu.VMEM((NX, BLOCK, rows), F32),
@@ -306,10 +330,11 @@
             collective_id=0, has_side_effects=True, vmem_limit_bytes=56 * 2**20),
         cost_estimate=pl.CostEstimate(
             flops=2 * rows * cs * width * VIRT * BLOCK, bytes_accessed=13 * 2**20, transcendentals=0),
-    )(amplitudes, integrals, jnp.transpose(mask, (1, 2, 0)), slab, owner.reshape(-1, 128))
-
-
-def solution(mesh, slots=24):
+    )(amplitudes, integrals.reshape(32, 32, cs, width), jnp.transpose(mask, (1, 2, 0)), slab, owner.reshape(-1, 128))
+    return own + fetched
+
+
+def solution(mesh, slots=17):
     return jax.shard_map(
         functools.partial(per_device, mesh.shape["pair"], slots),
         mesh=mesh,

time: 52.3 us -> 38.6 us (0.74)
  Pallas kernels: 49.3 us -> 36 us
  other arithmetic: 0 us -> 1.76 us
  local copies, waits for them, and re-layouts: 1.67 us -> 0 us
    pallas_call x1, Pallas kernels: 49.3 us -> 36 us  [per_device(): pl.pallas_call(functools.partial(kernel, n_pair, slots), out_shape=[jax.S...]
    add x0 -> x1, other arithmetic: none -> 1.76 us  [per_device(): return own + fetched]
    unnamed x1 -> x0, local copies, waits for them, and re-layouts: 1.67 us -> none
where the time goes in v3:
time: 38.6 us; the launch traced here: 38.5 us
  Pallas kernels  36 us (93%)
  other arithmetic  1.76 us (5%)
  between operations  0.66 us (2%)
    pallas_call x1, Pallas kernels, per_device(): pl.pallas_call(functools.partial(kernel, n_pair, slots), out_shape=[jax.S...  36 us
    add x1, other arithmetic, per_device(): return own + fetched  1.76 us

profile of v3, /device:TPU:1, one launch (start us, length us, event | category | flops | bytes accessed | tf_op | source)
XLA Modules:
  0.0 38.5 jit_solution(11525060360566620650)
XLA Ops:
  0.7 36.0 %shard_map.55 = (f32[512,128]{1,0:T(8,128)}, f32[512,128]{1,0:T(8,128)}) custom-call(bf16[512,16,256]{2,1,0:T(8,128)(2,1)} %amp.1, bf16[32,32,16,256]{3,2,1,0:T(8,128)(2,1)} %bitcast.3, s32[16,2,512]{2,1,0:T(2,128)} %bitcast.4, s32[1]{0:T(128)S(6)} %copy.6.slab_ref, s32[128,128]{1,0:T(8,128)} %bitcast.5), custom_call_target="tpu_custom_call" | custom-call | flops 4294967296 | bytes 13631488 | tf_op jit(solution)/shard_map/pallas_call | solution.py:291
  36.7 1.8 %add.3 = f32[512,128]{1,0:T(8,128)} add(f32[512,128]{1,0:T(8,128)} %get-tuple-element.7, f32[512,128]{1,0:T(8,128)} %get-tuple-element.8) | non-fusion elementwise | flops 65536 | bytes 786432 | tf_op jit(solution)/shard_map/add | solution.py:334

commit v4 on v3

v4 whole, which is shorter than its diff:
```python
import functools

import jax
import jax.numpy as jnp
from jax import lax
from jax.experimental import pallas as pl
from jax.experimental.pallas import tpu as pltpu
from jax.sharding import PartitionSpec as P

MESH = pl.DeviceIdType.MESH
F32 = jnp.float32
BF16 = jnp.bfloat16
NX = 4
CORES = 2
VIRT = NX * CORES
BLOCK = 128
PAD = 24
NZ = 8
SPAN = 256
HALF = BLOCK // 2
GROUPS = 2
NT = (((1,), (1,)), ((), ()))
NN = (((1,), (0,)), ((), ()))


def split_two(value):
    high = value.astype(BF16)
    return high, (value - high.astype(F32)).astype(BF16)


def iota(shape, dim):
    return lax.broadcasted_iota(jnp.int32, shape, dim)


def flatten_into(dst, row, block, cs, width):
    flat = pltpu.einshape("pcd->p(cd)", block)
    for j in range(2):
        for c in range(cs):
            at = j * cs * 128 + c * 128
            dst[pl.ds(row, 16), at:at + 128] = flat[:, c * width + j * 128:c * width + (j + 1) * 128]


def kernel(
    n_pair, slots,
    amp, ints, mask, slab_ref, owner, out,
    amp_raw, amp_flat, int_raw, int_flat, part, chip_in, acc, fwd, fin_left, fin_right,
    turned, partial, sent, came, send_one, take_one, mask_ref, owner_ref, result,
    amp_sem, int_sem, small_sem, out_sem,
    chip_send, chip_recv, ring_send, ring_recv, turn_send, turn_recv, pair_send, pair_recv,
):
    rows, cs, width = amp_raw.shape
    tiles = rows // 128
    half_k = cs * 128
    spans = rows // SPAN
    me_p = lax.axis_index("pair")
    me_v = lax.axis_index("virt")
    x = me_v // CORES
    core = me_v % CORES
    other = me_v + 1 - 2 * core
    right = ((x + 1) % NX) * CORES + core
    left = ((x + NX - 1) % NX) * CORES + core

    def fetch_amp(q):
        at = pl.ds(q * 128, 128)
        return pltpu.make_async_copy(amp.at[at], amp_raw.at[at], amp_sem.at[q])

    def fetch_ints(s):
        to = (x + (2, 1, 3, 0)[s]) % NX
        return pltpu.make_async_copy(ints.at[:, pl.ds(to * CORES * 4, CORES * 4)], int_raw.at[s], int_sem.at[s])

    fetch_mask = pltpu.make_async_copy(mask, mask_ref, small_sem.at[0])
    fetch_owner = pltpu.make_async_copy(owner, owner_ref, small_sem.at[1])
    fetch_amp(0).start()
    fetch_amp(1).start()
    fetch_ints(0).start()
    fetch_mask.start()
    for q in range(2, tiles):
        fetch_amp(q).start()
    for s in range(1, NX):
        fetch_ints(s).start()
    fetch_owner.start()

    barrier = pltpu.get_barrier_semaphore()

    @pl.loop(1, VIRT)
    def _(i):
        pl.semaphore_signal(barrier, inc=1, device_id=(me_p, (me_v + i) % VIRT), device_id_type=MESH)

    @pl.loop(1, n_pair)
    def _(i):
        pl.semaphore_signal(barrier, inc=1, device_id=((me_p + i) % n_pair, me_v), device_id_type=MESH)

    def arrange_amp(q):
        fetch_amp(q).wait()

        @pl.loop(0, 8, unroll=4)
        def _(g):
            row = pl.multiple_of(q * 128 + g * 16, 16)
            flatten_into(amp_flat, row, amp_raw[pl.ds(row, 16)], cs, width)

    runs = (((0, 0), (0, 4)), ((1, 4), (2, 0)), ((1, 0), (2, 4)), ((3, 0), (3, 4)))

    def arrange(k):
        flat = int_flat.at[k % 2]
        for c in range(CORES):
            for r in range(2):
                s, first = runs[k][r]

                @pl.loop(0, 4, unroll=4)
                def _(g):
                    block = jnp.concatenate(
                        [int_raw[s, (first + g) * 4 + a, pl.ds(c * 4, 4)] for a in range(4)], axis=0)
                    row = pl.multiple_of((c * 8 + r * 4 + g) * 16, 16)
                    flatten_into(flat, row, block, cs, width)

    def multiply(k, nb):
        flat = int_flat.at[k % 2]
        ps = slice(nb * SPAN, (nb + 1) * SPAN)
        one = lax.dot_general(flat[:, :half_k], amp_flat[ps, :half_k], NT, preferred_element_type=F32)
        two = lax.dot_general(flat[:, half_k:], amp_flat[ps, half_k:], NT, preferred_element_type=F32)
        value = one * select[0:1, ps] + two * select[1:2, ps]
        for c in range(CORES):
            part[k, nb, c] = value[c * BLOCK:(c + 1) * BLOCK]
        if k == 0 and nb == 0:
            pl.semaphore_wait(barrier, VIRT - 1 + n_pair - 1)
        chip_copy(k, nb).start()

    def chip_copy(k, nb):
        return pltpu.make_async_remote_copy(
            src_ref=part.at[k, nb, 1 - core], dst_ref=chip_in.at[k, nb],
            send_sem=chip_send.at[k, nb], recv_sem=chip_recv.at[k, nb],
            device_id=(me_p, other), device_id_type=MESH)

    def ring_copy(i, nb, src, dst, to):
        return pltpu.make_async_remote_copy(
            src_ref=src, dst_ref=dst, send_sem=ring_send.at[i, nb], recv_sem=ring_recv.at[i, nb],
            device_id=(me_p, to), device_id_type=MESH)

    low, high = pl.ds(0, HALF), pl.ds(HALF, HALF)
    ring = [[
        ring_copy(0, nb, acc.at[0, nb, low], fwd.at[0, nb], right),
        ring_copy(1, nb, acc.at[0, nb, high], fwd.at[1, nb], left),
        ring_copy(2, nb, acc.at[1, nb, low], fin_left.at[nb, high], right),
        ring_copy(3, nb, acc.at[1, nb, high], fin_right.at[nb, low], left),
        ring_copy(4, nb, acc.at[2, nb, low], fin_left.at[nb, low], right),
        ring_copy(5, nb, acc.at[2, nb, high], fin_right.at[nb, high], left),
    ] for nb in range(spans)]

    def chip_sum(k, nb):
        chip_copy(k, nb).wait_recv()
        acc[k, nb] = part[k, nb, core] + chip_in[k, nb]

    def send_direct(k, nb):
        chip_sum(k, nb)
        ring[nb][2 * k].start()
        ring[nb][2 * k + 1].start()

    def send_forward(nb):
        chip_sum(2, nb)
        ring[nb][0].wait_recv()
        acc[2, nb, low] += fwd[0, nb]
        ring[nb][4].start()
        ring[nb][1].wait_recv()
        acc[2, nb, high] += fwd[1, nb]
        ring[nb][5].start()

    arrange_amp(0)
    arrange_amp(1)
    fetch_ints(0).wait()
    arrange(0)
    fetch_mask.wait()
    select = mask_ref[slab_ref[0] // 8].astype(F32)
    multiply(0, 0)
    arrange_amp(2)
    arrange_amp(3)
    multiply(0, 1)
    send_direct(0, 0)
    fetch_ints(1).wait()
    fetch_ints(2).wait()
    arrange(1)
    send_direct(0, 1)
    multiply(1, 0)
    multiply(1, 1)
    arrange(2)
    send_direct(1, 0)
    multiply(2, 0)
    send_direct(1, 1)
    multiply(2, 1)
    fetch_ints(3).wait()
    arrange(3)
    send_forward(0)
    multiply(3, 0)
    send_forward(1)
    multiply(3, 1)
    fetch_owner.wait()

    eye = iota((128, 128), 0) == iota((128, 128), 1)

    def as_column(row):
        return jnp.sum(jnp.where(eye, row, 0.0), axis=1, keepdims=True)

    def as_row(column):
        return jnp.sum(jnp.where(eye, column, 0.0), axis=0, keepdims=True)

    own_rows = [owner_ref[pl.ds(me_p * tiles + t, 1), :] for t in range(tiles)]
    wanted = [as_column((r ^ 1).astype(F32)).astype(jnp.int32) for r in own_rows]
    order_rows = [(r // 2).astype(F32) for r in own_rows]
    order_columns = [as_column(r) for r in order_rows]
    there_columns = []
    for t in range(tiles):
        want = jnp.broadcast_to(wanted[t], (128, 128))

        def look(g, found):
            return jnp.where(owner_ref[pl.ds(g, 1), :] == want, g // tiles, found)

        found = lax.fori_loop(0, n_pair * tiles, look, jnp.zeros((128, 128), jnp.int32), unroll=4)
        there_columns.append(jnp.max(found.astype(F32), axis=1, keepdims=True))
    there_rows = [as_row(c) for c in there_columns]

    steps = [(dy, dz) for dy in range(n_pair // NZ) for dz in range(NZ) if dy or dz]
    steps.sort(key=lambda s: (-min(s[0], n_pair // NZ - s[0]) - min(s[1], NZ - s[1]), s))
    me_y, me_z = me_p // NZ, me_p % NZ

    def number(code):
        found = jnp.zeros(code.shape, jnp.int32)
        for i, (dy, dz) in enumerate(steps):
            found = jnp.where(code == dy * NZ + dz, i, found)
        return found

    n_slots = n_pair * PAD
    for t in range(tiles):
        before = jnp.zeros((128, 128), F32)
        for u in range(tiles):
            hit = (there_rows[u] == there_columns[t]) & (order_rows[u] < order_columns[t])
            before = before + jnp.where(hit, 1.0, 0.0)
        rank = as_row(jnp.sum(before, axis=1, keepdims=True)).astype(jnp.int32)
        there = there_rows[t].astype(jnp.int32)
        y, z = there // NZ, there % NZ
        ahead = ((y - me_y + n_pair) % (n_pair // NZ)) * NZ + (z - me_z + NZ) % NZ
        behind = ((me_y - y + n_pair) % (n_pair // NZ)) * NZ + (me_z - z + NZ) % NZ
        at = slice(t * 128, (t + 1) * 128)
        row = number(ahead) * PAD + rank
        send_one[:, at] = jnp.where(iota((n_slots, 128), 0) == row, 1.0, 0.0).astype(BF16)
        column = as_column((number(behind) * PAD + rank).astype(F32)).astype(jnp.int32)
        take_one[at, :] = jnp.where(iota((128, n_slots), 1) == column, 1.0, 0.0).astype(BF16)

    came[n_pair - 1] = jnp.zeros((slots, BLOCK), F32)
    source, target = iota((BLOCK, BLOCK), 0), iota((BLOCK, BLOCK), 1)
    group, first, second = source // 16, (source // 4) % 4, source % 4
    own_lanes = jnp.where(target == first * 32 + group * 4 + second, 1.0, 0.0).astype(BF16)
    mirror_lanes = jnp.where(target == second * 32 + group * 4 + first, 1.0, 0.0).astype(BF16)
    own_lanes = jnp.concatenate([own_lanes, own_lanes], axis=0)
    mirror_lanes = jnp.concatenate([mirror_lanes, mirror_lanes], axis=0)
    diagonal = jnp.where(iota((SPAN, SPAN), 0) == iota((SPAN, SPAN), 1), 1.0, 0.0).astype(BF16)

    def finish(nb):
        chip_sum(3, nb)
        for i in range(2, 6):
            ring[nb][i].wait_recv()
        value = acc[3, nb] + fin_left[nb] + fin_right[nb]
        acc[3, nb] = value
        return jnp.concatenate(split_two(value), axis=0)

    def pair_copy(i):
        dy, dz = steps[i]
        to = ((me_y + dy) % (n_pair // NZ)) * NZ + (me_z + dz) % NZ
        return pltpu.make_async_remote_copy(
            src_ref=sent.at[i], dst_ref=came.at[i], send_sem=pair_send.at[i], recv_sem=pair_recv.at[i],
            device_id=(to, me_v), device_id_type=MESH)

    partial[...] = lax.dot_general(send_one[:, :SPAN], finish(0), NT, preferred_element_type=F32)
    rest = finish(1)
    eighth = n_pair // 4
    for g in range(4):
        at = slice(g * eighth * PAD, (g + 1) * eighth * PAD)
        both = partial[at, :] + lax.dot_general(send_one[at, SPAN:], rest, NT, preferred_element_type=F32)
        sent[g * eighth:(g + 1) * eighth] = (both[:, :BLOCK] + both[:, BLOCK:]).reshape(eighth, PAD, BLOCK)[:, :slots]
        for i in range(g * eighth, min((g + 1) * eighth, n_pair - 1)):
            pair_copy(i).start()

    def turn_copy(i):
        to = (me_v + i) % VIRT
        src = acc.at[3, :, pl.ds(pl.multiple_of(to * 16, 16), 16)]
        dst = turned.at[:, pl.ds(pl.multiple_of(me_v * 16, 16), 16)]
        return pltpu.make_async_remote_copy(
            src_ref=src, dst_ref=dst, send_sem=turn_send.at[i], recv_sem=turn_recv.at[i],
            device_id=(me_p, to), device_id_type=MESH)

    for i in range(1, VIRT):
        turn_copy(i).start()
    mine = pl.ds(pl.multiple_of(me_v * 16, 16), 16)
    for nb in range(spans):
        turned[nb, mine, :] = acc[3, nb, mine, :]
    for i in range(1, VIRT):
        turn_copy(i).wait_recv()
    for nb in range(spans):
        at = slice(nb * SPAN, (nb + 1) * SPAN)
        own = lax.dot_general(
            diagonal, jnp.concatenate(split_two(turned[nb]), axis=0), NT, preferred_element_type=F32)
        result[at, :] = lax.dot_general(own.astype(BF16), own_lanes, NN, preferred_element_type=F32)

    def out_copy(t):
        at = pl.ds(t * 128, 128)
        return pltpu.make_async_copy(result.at[at], out.at[at], out_sem.at[t])

    some = n_pair // GROUPS
    pad = jnp.zeros((some, PAD - slots, BLOCK), F32)
    for g in range(GROUPS):
        for i in range(g * some, min((g + 1) * some, n_pair - 1)):
            pair_copy(i).wait_recv()
        rows_in = jnp.concatenate([came[g * some:(g + 1) * some], pad], axis=1).reshape(some * PAD, BLOCK)
        rows_in = jnp.concatenate(split_two(rows_in), axis=1)
        for t in range(tiles):
            at = slice(t * 128, (t + 1) * 128)
            fetched = lax.dot_general(
                take_one[at, g * some * PAD:(g + 1) * some * PAD], rows_in, NN, preferred_element_type=F32)
            result[at, :] += lax.dot_general(fetched.astype(BF16), mirror_lanes, NN, preferred_element_type=F32)
            if g == GROUPS - 1:
                out_copy(t).start()
    for t in range(tiles):
        out_copy(t).wait()

    for nb in range(spans):
        for k in range(NX):
            chip_copy(k, nb).wait_send()
        for copy in ring[nb]:
            copy.wait_send()
    for i in range(1, VIRT):
        turn_copy(i).wait_send()
    for i in range(n_pair - 1):
        pair_copy(i).wait_send()


def per_device(n_pair, slots, amplitudes, integrals, mask, slab, owner):
    rows, cs, width = amplitudes.shape
    dma = pltpu.SemaphoreType.DMA
    n_slots = n_pair * PAD
    spans = rows // SPAN
    anywhere = pl.BlockSpec(memory_space=pl.ANY)
    return pl.pallas_call(
        functools.partial(kernel, n_pair, slots),
        out_shape=jax.ShapeDtypeStruct((rows, BLOCK), F32),
        in_specs=[anywhere, anywhere, anywhere, pl.BlockSpec(memory_space=pltpu.SMEM), anywhere],
        out_specs=anywhere,
        scratch_shapes=[
            pltpu.VMEM((rows, cs, width), BF16),
            pltpu.VMEM((rows, cs * width), BF16),
            pltpu.VMEM((NX, 32, CORES * 4, cs, width), BF16),
            pltpu.VMEM((2, CORES * BLOCK, cs * width), BF16),
            pltpu.VMEM((NX, spans, CORES, BLOCK, SPAN), F32),
            pltpu.VMEM((NX, spans, BLOCK, SPAN), F32),
            pltpu.VMEM((NX, spans, BLOCK, SPAN), F32),
            pltpu.VMEM((2, spans, HALF, SPAN), F32),
            pltpu.VMEM((spans, BLOCK, SPAN), F32),
            pltpu.VMEM((spans, BLOCK, SPAN), F32),
            pltpu.VMEM((spans, BLOCK, SPAN), F32),
            pltpu.VMEM((n_slots, 2 * BLOCK), F32),
            pltpu.VMEM((n_pair, slots, BLOCK), F32),
            pltpu.VMEM((n_pair, slots, BLOCK), F32),
            pltpu.VMEM((n_slots, rows), BF16),
            pltpu.VMEM((rows, n_slots), BF16),
            pltpu.VMEM((16, 2, rows), jnp.int32),
            pltpu.VMEM((n_pair * rows // 128, 128), jnp.int32),
            pltpu.VMEM((rows, BLOCK), F32),
            dma((rows // 128,)),
            dma((NX,)),
            dma((2,)),
            dma((rows // 128,)),
            dma((NX, spans)),
            dma((NX, spans)),
            dma((6, spans)),
            dma((6, spans)),
            dma((VIRT,)),
            dma((VIRT,)),
            dma((n_pair,)),
            dma((n_pair,)),
        ],
        compiler_params=pltpu.CompilerParams(
            collective_id=0, has_side_effects=True, vmem_limit_bytes=56 * 2**20),
        cost_estimate=pl.CostEstimate(
            flops=2 * rows * cs * width * VIRT * BLOCK, bytes_accessed=13 * 2**20, transcendentals=0),
    )(amplitudes, integrals.reshape(32, 32, cs, width), jnp.transpose(mask, (1, 2, 0)), slab, owner.reshape(-1, 128))


def solution(mesh, slots=17):
    return jax.shard_map(
        functools.partial(per_device, mesh.shape["pair"], slots),
        mesh=mesh,
        in_specs=(
            P("pair", None, "virt"),
            P(None, None, "virt"),
            P("pair", None, "virt"),
            P(),
            P(),
        ),
        out_specs=P("pair", "virt"),
        check_vma=False,
    )
```

time: 38.6 us -> 39.6 us (1.026)
  other arithmetic: 1.76 us -> 0 us
  local copies, waits for them, and re-layouts: 0 us -> 1.67 us
  Pallas kernels: 36 us -> 37.2 us
    add x1 -> x0, other arithmetic: 1.76 us -> none  [per_device(): return own + fetched]
    unnamed x0 -> x1, local copies, waits for them, and re-layouts: none -> 1.67 us
    pallas_call x1, Pallas kernels: 36 us -> 37.2 us  [per_device(): pl.pallas_call(functools.partial(kernel, n_pair, slots), out_shape=jax.Sh...]
where the time goes in v4:
time: 39.6 us; the launch traced here: 39.5 us
  Pallas kernels  37.2 us (94%)
  local copies, waits for them, and re-layouts  1.67 us (4%)
  between operations  0.66 us (2%)
    pallas_call x1, Pallas kernels, per_device(): pl.pallas_call(functools.partial(kernel, n_pair, slots), out_shape=jax.Sh...  37.2 us
    unnamed x1, local copies, waits for them, and re-layouts  1.67 us

profile of v4, /device:TPU:1, one launch (start us, length us, event | category | flops | bytes accessed | tf_op | source)
XLA Modules:
  0.0 39.5 jit_solution(8553054869808391438)
XLA Ops:
  0.7 37.2 %shard_map.55 = f32[512,128]{1,0:T(8,128)} custom-call(bf16[512,16,256]{2,1,0:T(8,128)(2,1)} %amp.1, bf16[32,32,16,256]{3,2,1,0:T(8,128)(2,1)} %bitcast.3, s32[16,2,512]{2,1,0:T(2,128)} %bitcast.4, s32[1]{0:T(128)S(6)} %copy.7.slab_ref, s32[128,128]{1,0:T(8,128)} %bitcast.5), custom_call_target="tpu_custom_call" | custom-call | flops 4294967296 | bytes 13631488 | tf_op jit(solution)/shard_map/pallas_call | solution.py:340
  37.8 1.7 %copy.8 = f32[512,128]{1,0:T(8,128)} copy(f32[512,128]{1,0:T(8,128)} %shard_map.55) | data formatting | bytes 524288

commit v5 on v4

--- a/solution.py
+++ b/solution.py
@@ -44,9 +44,9 @@
     n_pair, slots,
     amp, ints, mask, slab_ref, owner, out,
     amp_raw, amp_flat, int_raw, int_flat, part, chip_in, acc, fwd, fin_left, fin_right,
-    turned, partial, sent, came, send_one, take_one, mask_ref, owner_ref, result,
+    turned, partial, sent, came, send_one, take_one, mask_ref, owner_ref, result, looks,
     amp_sem, int_sem, small_sem, out_sem,
-    chip_send, chip_recv, ring_send, ring_recv, turn_send, turn_recv, pair_send, pair_recv,
+    chip_send, chip_recv, ring_send, ring_recv, turn_send, turn_recv, pair_send, pair_recv, look_send, look_recv,
 ):
     rows, cs, width = amp_raw.shape
     tiles = rows // 128
@@ -163,6 +163,38 @@
         ring[nb][1].wait_recv()
         acc[2, nb, high] += fwd[1, nb]
         ring[nb][5].start()
+
+    eye = iota((128, 128), 0) == iota((128, 128), 1)
+
+    def as_column(row):
+        return jnp.sum(jnp.where(eye, row, 0.0), axis=1, keepdims=True)
+
+    def as_row(column):
+        return jnp.sum(jnp.where(eye, column, 0.0), axis=0, keepdims=True)
+
+    def look_copy(i):
+        return pltpu.make_async_remote_copy(
+            src_ref=looks.at[me_v], dst_ref=looks.at[me_v], send_sem=look_send.at[i], recv_sem=look_recv.at[i],
+            device_id=(me_p, (me_v + i) % VIRT), device_id_type=MESH)
+
+    share = n_pair * tiles // VIRT
+
+    def search():
+        fetch_owner.wait()
+        found_rows = []
+        for t in range(tiles):
+            row = owner_ref[pl.ds(me_p * tiles + t, 1), :]
+            want = jnp.broadcast_to(as_column((row ^ 1).astype(F32)).astype(jnp.int32), (128, 128))
+
+            def look(i, found):
+                g = me_v * share + i
+                return jnp.where(owner_ref[pl.ds(g, 1), :] == want, g // tiles, found)
+
+            found = lax.fori_loop(0, share, look, jnp.zeros((128, 128), jnp.int32), unroll=4)
+            found_rows.append(as_row(jnp.max(found.astype(F32), axis=1, keepdims=True)))
+        looks[me_v] = jnp.concatenate(found_rows + [jnp.zeros((8 - tiles, 128), F32)], axis=0)
+        for i in range(1, VIRT):
+            look_copy(i).start()
 
     arrange_amp(0)
     arrange_amp(1)
@@ -185,6 +217,7 @@
     send_direct(1, 0)
     multiply(2, 0)
     send_direct(1, 1)
+    search()
     multiply(2, 1)
     fetch_ints(3).wait()
     arrange(3)
@@ -192,30 +225,17 @@
     multiply(3, 0)
     send_forward(1)
     multiply(3, 1)
-    fetch_owner.wait()
-
-    eye = iota((128, 128), 0) == iota((128, 128), 1)
-
-    def as_column(row):
-        return jnp.sum(jnp.where(eye, row, 0.0), axis=1, keepdims=True)
-
-    def as_row(column):
-        return jnp.sum(jnp.where(eye, column, 0.0), axis=0, keepdims=True)
-
-    own_rows = [owner_ref[pl.ds(me_p * tiles + t, 1), :] for t in range(tiles)]
-    wanted = [as_column((r ^ 1).astype(F32)).astype(jnp.int32) for r in own_rows]
-    order_rows = [(r // 2).astype(F32) for r in own_rows]
+
+    for i in range(1, VIRT):
+        look_copy(i).wait_recv()
+    there_all = looks[0]
+    for v in range(1, VIRT):
+        there_all = there_all + looks[v]
+    there_rows = [there_all[t:t + 1] for t in range(tiles)]
+    there_columns = [as_column(r) for r in there_rows]
+    order_rows = [(owner_ref[pl.ds(me_p * tiles + t, 1), :] // 2).astype(F32) for t in range(tiles)]
     order_columns = [as_column(r) for r in order_rows]
-    there_columns = []
-    for t in range(tiles):
-        want = jnp.broadcast_to(wanted[t], (128, 128))
-
-        def look(g, found):
-            return jnp.where(owner_ref[pl.ds(g, 1), :] == want, g // tiles, found)
-
-        found = lax.fori_loop(0, n_pair * tiles, look, jnp.zeros((128, 128), jnp.int32), unroll=4)
-        there_columns.append(jnp.max(found.astype(F32), axis=1, keepdims=True))
-    there_rows = [as_row(c) for c in there_columns]
+
 
     steps = [(dy, dz) for dy in range(n_pair // NZ) for dz in range(NZ) if dy or dz]
     steps.sort(key=lambda s: (-min(s[0], n_pair // NZ - s[0]) - min(s[1], NZ - s[1]), s))
@@ -303,6 +323,15 @@
         at = pl.ds(t * 128, 128)
         return pltpu.make_async_copy(result.at[at], out.at[at], out_sem.at[t])
 
+    for nb in range(spans):
+        for k in range(NX):
+            chip_copy(k, nb).wait_send()
+        for copy in ring[nb]:
+            copy.wait_send()
+    for i in range(1, VIRT):
+        turn_copy(i).wait_send()
+        look_copy(i).wait_send()
+
     some = n_pair // GROUPS
     pad = jnp.zeros((some, PAD - slots, BLOCK), F32)
     for g in range(GROUPS):
@@ -317,18 +346,10 @@
             result[at, :] += lax.dot_general(fetched.astype(BF16), mirror_lanes, NN, preferred_element_type=F32)
             if g == GROUPS - 1:
                 out_copy(t).start()
+    for i in range(n_pair - 1):
+        pair_copy(i).wait_send()
     for t in range(tiles):
         out_copy(t).wait()
-
-    for nb in range(spans):
-        for k in range(NX):
-            chip_copy(k, nb).wait_send()
-        for copy in ring[nb]:
-            copy.wait_send()
-    for i in range(1, VIRT):
-        turn_copy(i).wait_send()
-    for i in range(n_pair - 1):
-        pair_copy(i).wait_send()
 
 
 def per_device(n_pair, slots, amplitudes, integrals, mask, slab, owner):
@@ -362,6 +383,7 @@
             pltpu.VMEM((16, 2, rows), jnp.int32),
             pltpu.VMEM((n_pair * rows // 128, 128), jnp.int32),
             pltpu.VMEM((rows, BLOCK), F32),
+            pltpu.VMEM((VIRT, 8, 128), F32),
             dma((rows // 128,)),
             dma((NX,)),
             dma((2,)),
@@ -374,6 +396,8 @@
             dma((VIRT,)),
             dma((n_pair,)),
             dma((n_pair,)),
+            dma((VIRT,)),
+            dma((VIRT,)),
         ],
         compiler_params=pltpu.CompilerParams(
             collective_id=0, has_side_effects=True, vmem_limit_bytes=56 * 2**20),

time: 39.6 us -> 39.2 us (0.990)
  Pallas kernels: 37.2 us -> 36.7 us
    pallas_call x1, Pallas kernels: 37.2 us -> 36.7 us  [per_device(): pl.pallas_call(functools.partial(kernel, n_pair, slots), out_shape=jax.Sh...]
where the time goes in v5:
time: 39.2 us; the launch traced here: 39 us
  Pallas kernels  36.7 us (94%)
  local copies, waits for them, and re-layouts  1.67 us (4%)
  between operations  0.66 us (2%)
    pallas_call x1, Pallas kernels, per_device(): pl.pallas_call(functools.partial(kernel, n_pair, slots), out_shape=jax.Sh...  36.7 us
    unnamed x1, local copies, waits for them, and re-layouts  1.67 us

profile of v5, /device:TPU:1, one launch (start us, length us, event | category | flops | bytes accessed | tf_op | source)
XLA Modules:
  0.0 39.0 jit_solution(9048605841479791998)
XLA Ops:
  0.7 36.7 %shard_map.55 = f32[512,128]{1,0:T(8,128)} custom-call(bf16[512,16,256]{2,1,0:T(8,128)(2,1)} %amp.1, bf16[32,32,16,256]{3,2,1,0:T(8,128)(2,1)} %bitcast.3, s32[16,2,512]{2,1,0:T(2,128)} %bitcast.4, s32[1]{0:T(128)S(6)} %copy.7.slab_ref, s32[128,128]{1,0:T(8,128)} %bitcast.5), custom_call_target="tpu_custom_call" | custom-call | flops 4294967296 | bytes 13631488 | tf_op jit(solution)/shard_map/pallas_call | solution.py:361
  37.4 1.7 %copy.8 = f32[512,128]{1,0:T(8,128)} copy(f32[512,128]{1,0:T(8,128)} %shard_map.55) | data formatting | bytes 524288

commit v6 on v5

--- a/solution.py
+++ b/solution.py
@@ -121,15 +121,21 @@
         value = one * select[0:1, ps] + two * select[1:2, ps]
         for c in range(CORES):
             part[k, nb, c] = value[c * BLOCK:(c + 1) * BLOCK]
-        if k == 0 and nb == 0:
-            pl.semaphore_wait(barrier, VIRT - 1 + n_pair - 1)
-        chip_copy(k, nb).start()
-
-    def chip_copy(k, nb):
+        if k == 0:
+            if nb == 0:
+                pl.semaphore_wait(barrier, VIRT - 1 + n_pair - 1)
+            chip_copy(k, pl.ds(nb, 1), nb).start()
+        elif nb == spans - 1:
+            chip_copy(k, pl.ds(0, spans), 0).start()
+
+    def chip_copy(k, at, i):
         return pltpu.make_async_remote_copy(
-            src_ref=part.at[k, nb, 1 - core], dst_ref=chip_in.at[k, nb],
-            send_sem=chip_send.at[k, nb], recv_sem=chip_recv.at[k, nb],
+            src_ref=part.at[k, at, 1 - core], dst_ref=chip_in.at[k, at],
+            send_sem=chip_send.at[k, i], recv_sem=chip_recv.at[k, i],
             device_id=(me_p, other), device_id_type=MESH)
+
+    every = pl.ds(0, spans)
+    chip_copies = [chip_copy(0, pl.ds(nb, 1), nb) for nb in range(spans)] + [chip_copy(k, every, 0) for k in range(1, NX)]
 
     def ring_copy(i, nb, src, dst, to):
         return pltpu.make_async_remote_copy(
@@ -137,32 +143,42 @@
             device_id=(me_p, to), device_id_type=MESH)
 
     low, high = pl.ds(0, HALF), pl.ds(HALF, HALF)
-    ring = [[
+    starts = [(
         ring_copy(0, nb, acc.at[0, nb, low], fwd.at[0, nb], right),
         ring_copy(1, nb, acc.at[0, nb, high], fwd.at[1, nb], left),
-        ring_copy(2, nb, acc.at[1, nb, low], fin_left.at[nb, high], right),
-        ring_copy(3, nb, acc.at[1, nb, high], fin_right.at[nb, low], left),
-        ring_copy(4, nb, acc.at[2, nb, low], fin_left.at[nb, low], right),
-        ring_copy(5, nb, acc.at[2, nb, high], fin_right.at[nb, high], left),
-    ] for nb in range(spans)]
-
-    def chip_sum(k, nb):
-        chip_copy(k, nb).wait_recv()
-        acc[k, nb] = part[k, nb, core] + chip_in[k, nb]
-
-    def send_direct(k, nb):
-        chip_sum(k, nb)
-        ring[nb][2 * k].start()
-        ring[nb][2 * k + 1].start()
-
-    def send_forward(nb):
-        chip_sum(2, nb)
-        ring[nb][0].wait_recv()
-        acc[2, nb, low] += fwd[0, nb]
-        ring[nb][4].start()
-        ring[nb][1].wait_recv()
-        acc[2, nb, high] += fwd[1, nb]
-        ring[nb][5].start()
+    ) for nb in range(spans)]
+    direct = (
+        ring_copy(2, 0, acc.at[1, every, low], fin_left.at[every, high], right),
+        ring_copy(3, 0, acc.at[1, every, high], fin_right.at[every, low], left),
+    )
+    forward = (
+        ring_copy(4, 0, acc.at[2, every, low], fin_left.at[every, low], right),
+        ring_copy(5, 0, acc.at[2, every, high], fin_right.at[every, high], left),
+    )
+
+    def send_start(nb):
+        chip_copies[nb].wait_recv()
+        acc[0, nb] = part[0, nb, core] + chip_in[0, nb]
+        for copy in starts[nb]:
+            copy.start()
+
+    def chip_sum(k):
+        chip_copies[spans + k - 1].wait_recv()
+        for nb in range(spans):
+            acc[k, nb] = part[k, nb, core] + chip_in[k, nb]
+
+    def send_direct():
+        chip_sum(1)
+        for copy in direct:
+            copy.start()
+
+    def send_forward():
+        chip_sum(2)
+        for side, piece in enumerate((low, high)):
+            for nb in range(spans):
+                starts[nb][side].wait_recv()
+                acc[2, nb, piece] += fwd[side, nb]
+            forward[side].start()
 
     eye = iota((128, 128), 0) == iota((128, 128), 1)
 
@@ -206,24 +222,22 @@
     arrange_amp(2)
     arrange_amp(3)
     multiply(0, 1)
-    send_direct(0, 0)
+    send_start(0)
     fetch_ints(1).wait()
     fetch_ints(2).wait()
     arrange(1)
-    send_direct(0, 1)
+    send_start(1)
     multiply(1, 0)
     multiply(1, 1)
     arrange(2)
-    send_direct(1, 0)
+    send_direct()
     multiply(2, 0)
-    send_direct(1, 1)
     search()
     multiply(2, 1)
     fetch_ints(3).wait()
     arrange(3)
-    send_forward(0)
     multiply(3, 0)
-    send_forward(1)
+    send_forward()
     multiply(3, 1)
 
     for i in range(1, VIRT):
@@ -274,9 +288,10 @@
     diagonal = jnp.where(iota((SPAN, SPAN), 0) == iota((SPAN, SPAN), 1), 1.0, 0.0).astype(BF16)
 
     def finish(nb):
-        chip_sum(3, nb)
-        for i in range(2, 6):
-            ring[nb][i].wait_recv()
+        if nb == 0:
+            chip_sum(3)
+            for copy in direct + forward:
+                copy.wait_recv()
         value = acc[3, nb] + fin_left[nb] + fin_right[nb]
         acc[3, nb] = value
         return jnp.concatenate(split_two(value), axis=0)
@@ -323,11 +338,8 @@
         at = pl.ds(t * 128, 128)
         return pltpu.make_async_copy(result.at[at], out.at[at], out_sem.at[t])
 
-    for nb in range(spans):
-        for k in range(NX):
-            chip_copy(k, nb).wait_send()
-        for copy in ring[nb]:
-            copy.wait_send()
+    for copy in chip_copies + [c for pair in starts for c in pair] + list(direct + forward):
+        copy.wait_send()
     for i in range(1, VIRT):
         turn_copy(i).wait_send()
         look_copy(i).wait_send()

time: 39.2 us -> 39.8 us (1.015)
  Pallas kernels: 36.7 us -> 37.4 us
    pallas_call x1, Pallas kernels: 36.7 us -> 37.4 us  [per_device(): pl.pallas_call(functools.partial(kernel, n_pair, slots), out_shape=jax.Sh...]
where the time goes in v6:
time: 39.8 us; the launch traced here: 39.7 us
  Pallas kernels  37.4 us (94%)
  local copies, waits for them, and re-layouts  1.67 us (4%)
  between operations  0.66 us (2%)
    pallas_call x1, Pallas kernels, per_device(): pl.pallas_call(functools.partial(kernel, n_pair, slots), out_shape=jax.Sh...  37.4 us
    unnamed x1, local copies, waits for them, and re-layouts  1.67 us

profile of v6, /device:TPU:1, one launch (start us, length us, event | category | flops | bytes accessed | tf_op | source)
XLA Modules:
  0.0 39.7 jit_solution(8464701257487977920)
XLA Ops:
  0.7 37.4 %shard_map.55 = f32[512,128]{1,0:T(8,128)} custom-call(bf16[512,16,256]{2,1,0:T(8,128)(2,1)} %amp.1, bf16[32,32,16,256]{3,2,1,0:T(8,128)(2,1)} %bitcast.3, s32[16,2,512]{2,1,0:T(2,128)} %bitcast.4, s32[1]{0:T(128)S(6)} %copy.7.slab_ref, s32[128,128]{1,0:T(8,128)} %bitcast.5), custom_call_target="tpu_custom_call" | custom-call | flops 4294967296 | bytes 13631488 | tf_op jit(solution)/shard_map/pallas_call | solution.py:373
  38.1 1.7 %copy.8 = f32[512,128]{1,0:T(8,128)} copy(f32[512,128]{1,0:T(8,128)} %shard_map.55) | data formatting | bytes 524288

commit v7 on v3

--- a/solution.py
+++ b/solution.py
@@ -15,6 +15,7 @@
 VIRT = NX * CORES
 BLOCK = 128
 PAD = 24
+NZ = 8
 NT = (((1,), (1,)), ((), ()))
 NN = (((1,), (0,)), ((), ()))
 
@@ -233,14 +234,17 @@
         send_one[...], jnp.concatenate([sum_high, sum_low], axis=0), NT, preferred_element_type=F32)
     sent[...] = (both[:, :BLOCK] + both[:, BLOCK:]).reshape(n_pair, PAD, BLOCK)[:, :slots]
 
+    steps = [(dy, dz) for dy in range(n_pair // NZ) for dz in range(NZ) if dy or dz]
+    steps.sort(key=lambda s: (-min(s[0], n_pair // NZ - s[0]) - min(s[1], NZ - s[1]), s))
+
     def pair_copy(i):
-        to = (me_p + i) % n_pair
+        dy, dz = steps[i]
+        to = ((me_p // NZ + dy) % (n_pair // NZ)) * NZ + (me_p + dz) % NZ
         return pltpu.make_async_remote_copy(
             src_ref=sent.at[to], dst_ref=came.at[me_p], send_sem=pair_send.at[i], recv_sem=pair_recv.at[i],
             device_id=(to, me_v), device_id_type=MESH)
 
-    @pl.loop(1, n_pair)
-    def _(i):
+    for i in range(n_pair - 1):
         pair_copy(i).start()
 
     def turn_copy(i):
@@ -261,26 +265,22 @@
     own_pair = lax.dot_general(diagonal, jnp.concatenate([own_high, own_low], axis=0), NT, preferred_element_type=F32)
     own_ref[...] = lax.dot_general(own_pair.astype(BF16), own_lanes, NN, preferred_element_type=F32)
 
-    @pl.loop(1, n_pair)
-    def _(i):
-        pair_copy(i).wait_recv()
-
-    rest = jnp.zeros((n_pair, PAD - slots, BLOCK), F32)
-    came_high, came_low = split_two(jnp.concatenate([came[...], rest], axis=1).reshape(n_slots, BLOCK))
-    fetched = lax.dot_general(
-        take_one[...], jnp.concatenate([came_high, came_low], axis=1), NN, preferred_element_type=F32)
-    fetched_ref[...] = lax.dot_general(fetched.astype(BF16), mirror_lanes, NN, preferred_element_type=F32)
-
     for k in range(NX):
         chip_copy(k).wait_send()
     for copy in ring:
         copy.wait_send()
     for i in range(1, VIRT):
         turn_copy(i).wait_send()
-
-    @pl.loop(1, n_pair)
-    def _(i):
+    for i in range(n_pair - 1):
         pair_copy(i).wait_send()
+    for i in range(n_pair - 1):
+        pair_copy(i).wait_recv()
+
+    rest = jnp.zeros((n_pair, PAD - slots, BLOCK), F32)
+    came_high, came_low = split_two(jnp.concatenate([came[...], rest], axis=1).reshape(n_slots, BLOCK))
+    fetched = lax.dot_general(
+        take_one[...], jnp.concatenate([came_high, came_low], axis=1), NN, preferred_element_type=F32)
+    fetched_ref[...] = lax.dot_general(fetched.astype(BF16), mirror_lanes, NN, preferred_element_type=F32)
 
 
 def per_device(n_pair, slots, amplitudes, integrals, mask, slab, owner):

time: 38.6 us -> 38.8 us (level)
  no operation moved by 1% of the time
where the time goes in v7:
time: 38.8 us; the launch traced here: 38.7 us
  Pallas kernels  36.2 us (93%)
  other arithmetic  1.76 us (5%)
  between operations  0.66 us (2%)
    pallas_call x1, Pallas kernels, per_device(): pl.pallas_call(functools.partial(kernel, n_pair, slots), out_shape=[jax.S...  36.2 us
    add x1, other arithmetic, per_device(): return own + fetched  1.76 us

profile of v7, /device:TPU:1, one launch (start us, length us, event | category | flops | bytes accessed | tf_op | source)
XLA Modules:
  0.0 38.7 jit_solution(2643923505695739454)
XLA Ops:
  0.7 36.2 %shard_map.55 = (f32[512,128]{1,0:T(8,128)}, f32[512,128]{1,0:T(8,128)}) custom-call(bf16[512,16,256]{2,1,0:T(8,128)(2,1)} %amp.1, bf16[32,32,16,256]{3,2,1,0:T(8,128)(2,1)} %bitcast.3, s32[16,2,512]{2,1,0:T(2,128)} %bitcast.4, s32[1]{0:T(128)S(6)} %copy.6.slab_ref, s32[128,128]{1,0:T(8,128)} %bitcast.5), custom_call_target="tpu_custom_call" | custom-call | flops 4294967296 | bytes 13631488 | tf_op jit(solution)/shard_map/pallas_call | solution.py:291
  36.9 1.8 %add.3 = f32[512,128]{1,0:T(8,128)} add(f32[512,128]{1,0:T(8,128)} %get-tuple-element.7, f32[512,128]{1,0:T(8,128)} %get-tuple-element.8) | non-fusion elementwise | flops 65536 | bytes 786432 | tf_op jit(solution)/shard_map/add | solution.py:334
